TPU v7x, 32 devices: a whole 2x2x4 slice. The times are simulated.
32 devices in a mesh: groups: 2 (over y), sol: 4 (over z), head: 2 (over x), sub: 2 (over core).
Axes of the slice: x: 2, y: 2, z: 4, core: 2. Of those that a mesh axis runs over, the one named last changes fastest.
Arguments:
- query_key: bfloat16 [16, 512, 2, 2048], P(('groups', 'sol'), None, None, ('head', 'sub')), parts along dimension 0, may hold values from -6 to 6
- values_in: bfloat16 [16, 512, 4096], P(('groups', 'sol'), None, ('head', 'sub')), parts along dimension 0, may hold values from -6 to 6
- gate_in: bfloat16 [16, 512, 4096], P(('groups', 'sol'), None, ('head', 'sub')), parts along dimension 0, may hold values from -6 to 6
- decay_in: float32 [16, 32, 512], P(('groups', 'sol'), ('head', 'sub')), parts along dimension 0, may hold values from -6 to 6
- beta_in: float32 [16, 32, 512], P(('groups', 'sol'), ('head', 'sub')), parts along dimension 0, may hold values from -6 to 6
- decay_rate: float32 [32], P(('head', 'sub')), may hold values from 0.002 to 0.08
- decay_bias: float32 [32], P(('head', 'sub')), may hold values from -1 to 1
- conv_qk: float32 [4, 2, 2048], P(None, None, ('head', 'sub')), may hold values from -3 to 3
- conv_v: float32 [4, 4096], P(None, ('head', 'sub')), may hold values from -3 to 3
- prompt_states: bfloat16 [8, 32, 128, 128], P(('groups', 'sol'), ('head', 'sub')), parts along dimension 0, may hold values from -6 to 6
- prompt_of: int32 [16], P(('groups', 'sol')), parts along dimension 0, may hold values from 0 to 3
- step_ends: int32 [16, 2], P(('groups', 'sol')), parts along dimension 0, may hold values from 1 to 512, as said below
- norm_gain: float32 [128], replicated, may hold values from 0.25 to 1.75
- probe: bfloat16 [4096], replicated, may hold values from -0.09375 to 0.09375
Outputs:
- hidden: bfloat16 [16, 512, 4096], P(('groups', 'sol'), ('head', 'sub')), parts along dimension 0
- step_logits: float32 [16, 2], P(('groups', 'sol')), parts along dimension 0
There are 2 independent parts, one for each index of `groups`. A program takes and returns all parts, laid end to end along the dimension named above; an argument that names none is the same for every part. Nothing has to cross between parts.
Inputs may be any that keep to these rules, and one draw needn't show every extreme that they name: Solution s continues prompt prompt_of[s]. step_ends[s,0] < step_ends[s,1]; the first step covers positions below step_ends[s,0], the second the positions from there below step_ends[s,1]; later positions are padding. Some solution has step_ends[s,1] = 512.
All inputs are finite; a program needn't handle non-finite values.
Results may differ from a plain program's by a relative error of at most 0.0032.
Values may be sent and summed in bfloat16 or wider, within the bound.
A program may use at most 128 MiB of HBM per device.

v0:
```python
import jax
import jax.numpy as jnp
from jax import lax
from jax.sharding import PartitionSpec as P

BLOCK = 128


def conv_silu(inputs, kernel):
    width = kernel.shape[0]
    count = inputs.shape[1]
    padded = jnp.pad(inputs, ((0, 0), (width - 1, 0), (0, 0)))
    total = jnp.zeros(inputs.shape, jnp.float32)
    for offset in range(width):
        total = total + padded[:, offset : offset + count, :] * kernel[offset]
    return jax.nn.silu(total)


def unit_rows(field, head_size):
    shape = field.shape
    split = field.reshape(shape[:-1] + (shape[-1] // head_size, head_size))
    return split / jnp.sqrt(jnp.sum(split * split, axis=-1, keepdims=True) + 1e-06)


def pick_states(owners, block):
    labels = jnp.arange(block.shape[0], dtype=jnp.int32)
    select = (owners[:, None] == labels[None, :]).astype(jnp.bfloat16)
    return jnp.einsum("sp,phkv->shkv", select, block, preferred_element_type=jnp.float32)


def delta_blocks(queries, keys, values, log_decay, beta, initial):
    sols, length, heads, size = queries.shape
    count = length // BLOCK
    highest = lax.Precision.HIGHEST

    def blocks(field):
        return field.reshape(sols, count, BLOCK, heads, size).transpose(1, 0, 3, 2, 4)

    def gates(field):
        return field.reshape(sols, heads, count, BLOCK).transpose(2, 0, 1, 3)

    query_blocks = blocks(queries)
    key_blocks = blocks(keys)
    value_blocks = blocks(values)
    cumulative = jnp.cumsum(gates(log_decay), axis=-1)
    rate = gates(beta)
    places = jnp.arange(BLOCK)
    within = places[:, None] >= places[None, :]
    strict = places[:, None] > places[None, :]
    spread = cumulative[..., :, None] - cumulative[..., None, :]
    weights = jnp.where(within, jnp.exp(jnp.where(within, spread, 0.0)), 0.0)
    key_gram = jnp.einsum("nshid,nshjd->nshij", key_blocks, key_blocks, precision=highest)
    system = jnp.eye(BLOCK, dtype=jnp.float32) + jnp.where(
        strict, rate[..., :, None] * key_gram * weights, 0.0
    )
    right = jnp.concatenate(
        [rate[..., None] * value_blocks, (rate * jnp.exp(cumulative))[..., None] * key_blocks],
        axis=-1,
    )
    solved = jax.scipy.linalg.solve_triangular(system, right, lower=True, unit_diagonal=True)
    updates = solved[..., :size]
    corrections = solved[..., size:]
    scores = jnp.einsum("nshid,nshjd->nshij", query_blocks, key_blocks, precision=highest) * weights

    def advance(state, inputs):
        query, key, update, correction, score, cumul = inputs
        fresh = update - jnp.einsum("shck,shkv->shcv", correction, state, precision=highest)
        output = jnp.exp(cumul)[..., None] * jnp.einsum(
            "shck,shkv->shcv", query, state, precision=highest
        )
        output = output + jnp.einsum("shij,shjv->shiv", score, fresh, precision=highest)
        last = cumul[..., -1:]
        tail = jnp.exp(last - cumul)
        state = jnp.exp(last)[..., None] * state + jnp.einsum(
            "shck,shcv->shkv", key * tail[..., None], fresh, precision=highest
        )
        return (state, output)

    unused, outputs = lax.scan(
        advance, initial, (query_blocks, key_blocks, updates, corrections, scores, cumulative)
    )
    return outputs.transpose(1, 0, 3, 2, 4).reshape(sols, length, heads * size)


def gated_norm(core, gate, gain, first, ends):
    sols, count, width = core.shape
    size = gain.shape[0]
    split = core.reshape(sols, count, width // size, size)
    scale = jnp.sqrt(jnp.mean(split * split, axis=-1, keepdims=True) + 1e-06)
    normed = split / scale * gain * jax.nn.silu(gate.reshape(split.shape).astype(jnp.float32))
    places = first + jnp.arange(count, dtype=jnp.int32)
    live = places[None, :] < ends[:, 1:2]
    hidden = jnp.where(live[:, :, None], normed.reshape(sols, count, width), 0.0).astype(
        jnp.bfloat16
    )
    return (hidden, places)


def end_terms(hidden, probe_part, places, ends):
    sols, count, width = hidden.shape
    reward = jnp.dot(
        hidden.reshape(sols * count, width), probe_part, preferred_element_type=jnp.float32
    ).reshape(sols, count)
    marked = places[None, :, None] == (ends - 1)[:, None, :]
    return jnp.sum(jnp.where(marked, reward[:, :, None], 0.0), axis=1)


def shuffle_pair(core, gate):
    moved_core, moved_gate = (
        lax.all_to_all(core, ("head", "sub"), split_axis=1, concat_axis=2, tiled=True),
        lax.all_to_all(
            gate.astype(jnp.float32), ("head", "sub"), split_axis=1, concat_axis=2, tiled=True
        ).astype(gate.dtype),
    )
    return (moved_core, moved_gate)


def on_device(
    query_key,
    values_in,
    gate_in,
    decay_in,
    beta_in,
    decay_rate,
    decay_bias,
    conv_qk,
    conv_v,
    prompt_states,
    prompt_of,
    step_ends,
    norm_gain,
    probe,
):
    sols, length = (query_key.shape[0], query_key.shape[1])
    key_width = query_key.shape[3]
    head_size = prompt_states.shape[-1]
    value_heads = prompt_states.shape[1]
    mixed = conv_silu(
        query_key.reshape(sols, length, 2 * key_width),
        conv_qk.reshape(conv_qk.shape[0], 2 * key_width),
    )
    queries = unit_rows(mixed[:, :, :key_width], head_size) * head_size ** (-0.5)
    keys = unit_rows(mixed[:, :, key_width:], head_size)
    repeat = value_heads // queries.shape[2]
    queries = jnp.repeat(queries, repeat, axis=2)
    keys = jnp.repeat(keys, repeat, axis=2)
    values = conv_silu(values_in, conv_v).reshape(sols, length, value_heads, head_size)
    log_decay = -decay_rate[None, :, None] * jax.nn.softplus(decay_in + decay_bias[None, :, None])
    beta = jax.nn.sigmoid(beta_in)
    every = lax.all_gather(prompt_states, "sol", axis=0, tiled=True)
    initial = pick_states(prompt_of, every)
    core = delta_blocks(queries, keys, values, log_decay, beta, initial)
    moved_core, moved_gate = shuffle_pair(core, gate_in)
    share = length // lax.axis_size(("head", "sub"))
    hidden, places = gated_norm(
        moved_core, moved_gate, norm_gain, lax.axis_index(("head", "sub")) * share, step_ends
    )
    partial_value = end_terms(hidden, probe, places, step_ends)
    step_logits = lax.psum(partial_value, ("head", "sub"))
    return (hidden, step_logits)


def solution(mesh):
    return jax.shard_map(
        on_device,
        mesh=mesh,
        in_specs=(
            P(("groups", "sol"), None, None, ("head", "sub")),
            P(("groups", "sol"), None, ("head", "sub")),
            P(("groups", "sol"), None, ("head", "sub")),
            P(("groups", "sol"), ("head", "sub"), None),
            P(("groups", "sol"), ("head", "sub"), None),
            P(("head", "sub")),
            P(("head", "sub")),
            P(None, None, ("head", "sub")),
            P(None, ("head", "sub")),
            P(("groups", "sol"), ("head", "sub"), None, None),
            P(("groups", "sol")),
            P(("groups", "sol"), None),
            P(),
            P(),
        ),
        out_specs=(P(("groups", "sol"), ("head", "sub"), None), P(("groups", "sol"), None)),
        check_vma=False,
    )
```

profile of v0, /device:TPU:0, one launch (start us, length us, event | category | flops | bytes accessed | tf_op | source)
XLA Modules:
  0.0 896.1 jit_solution(11144132423608465836)
XLA Ops:
  7.9 5.1 copy.128
  13.0 4.8 all-to-all-start.1
  17.9 3.3 reshape.201
  21.2 2.8 divide_multiply_fusion.1
  31.4 2.8 divide_multiply_fusion
  34.2 2.9 copy.143
  42.1 11.1 %add_bitcast_fusion = f32[4,2,8,1,128,128]{5,4,3,2,1,0:T(8,128)} fusion(f32[128,128]{1,0:T(8,128)S(1)} %get-tuple-element.149, f32[4,2,8,128]{3,2,1,0:T(8,128)S(1)} %reduce_window_sum.11, f32[4,2,8,128]{3,2,1,0:T(8,128)S(1)} %copy_bitcast_fusion, f32[128,128]{1,0:T(8,128)S(1)} %get-tuple-element.148, pred[128,128]{1,0:T(8,128)(4,1)S(1)} %iota_compare_fusion.1, ...), kind=kOutput, calls=%fused_computation.44 | convolution fusion | flops 1620049920 | bytes 8634368 | tf_op jit(solution)/shard_map/nshid,nshjd->nshij/dot_general | solution.py:52
  53.2 630.3 %custom-call.4 = f32[4,2,8,1,128,128]{4,5,3,2,1,0:T(8,128)} custom-call(f32[4,2,8,1,128,128]{5,4,3,2,1,0:T(8,128)} %add_bitcast_fusion), custom_call_target="InvertDiagBlocksLowerTriangular" | custom-call | tf_op jit(solution)/shard_map/jit(_solve_triangular)/vmap(vmap(vmap()))/triangular_solve | solution.py:60
  693.6 5.2 bitcast_multiply_fusion.3
  698.8 10.3 %fusion.12 = f32[4,2,8,128,256]{4,3,2,1,0:T(8,128)S(1)} fusion(f32[4,2,8,128,128]{4,3,2,1,0:T(8,128)S(1)} %get-tuple-element.151, f32[4,2,8,128,128]{4,3,2,1,0:T(8,128)S(1)} %get-tuple-element.150, f32[4,2,8,1,128,128]{4,5,3,2,1,0:T(8,128)} %custom-call.4), kind=kOutput, calls=%fused_computation.23 | convolution fusion | flops 3223322624 | bytes 20971520 | tf_op jit(solution)/shard_map/jit(_solve_triangular)/vmap(vmap(vmap()))/triangular_solve | solution.py:60
  709.1 5.3 fusion.48
  715.5 10.6 %fusion.27 = f32[4,2,8,128,128]{4,3,2,1,0:T(8,128)} fusion(f32[4,2,8,128]{3,2,1,0:T(8,128)S(1)} %reduce_window_sum.11, pred[128,128]{1,0:T(8,128)(4,1)S(1)} %iota_compare_fusion.1, f32[2,4,128,8,128]{4,2,1,3,0:T(8,128)S(1)} %bitcast.180, f32[4,2,8,128,128]{4,3,0,2,1:T(8,128)S(1)} %bitcast.185), kind=kOutput, calls=%fused_computation.46 | convolution fusion | flops 1614807040 | bytes 12632064 | tf_op jit(solution)/shard_map/nshid,nshjd->nshij/dot_general | solution.py:63
  728.4 58.6 %while.13 = (s32[]{:T(128)}, f32[2,8,128,128]{3,2,1,0:T(8,128)S(1)}, f32[4,2,8,128,128]{4,3,2,1,0:T(8,128)}, f32[4,2,8,128]{3,2,1,0:T(8,128)S(1)}, f32[4,2,8,128...) while((s32[]{:T(128)}, ...), condition=%wide.region_4.5_spmd.clone, body=%wide.region_3.4_spmd.sunk.clone | while | flops 1612187648 | bytes 20032420 | solution.py:79
  731.3 2.8 convolution_subtract_fusion.3
  734.1 3.4 fusion.82
  745.9 2.8 convolution_subtract_fusion.3
  748.7 3.4 fusion.82
  760.6 2.8 convolution_subtract_fusion.3
  763.4 3.4 fusion.82
  775.2 2.8 convolution_subtract_fusion.3
  778.0 3.4 fusion.82
  787.0 6.6 copy.135
  793.5 5.8 reshape.212
  799.3 5.3 all-to-all-start
  805.0 6.7 copy.129
  811.7 41.7 %all-to-all-done = f32[2,512,1024]{2,0,1:T(2,128)} async-done(((f32[2,512,1024]{2,0,1:T(2,128)}), f32[2,512,1024]{2,0,1:T(2,128)}, u32[]{:S(2)}, u32[]{:S(2)}) %all-to-all-start) | async-done | bytes 4194336 | tf_op jit(solution)/shard_map/all_to_all | solution.py:110
  853.4 3.5 copy.125
  858.8 2.9 mul.258
  861.7 5.4 copy.126
  867.1 5.4 copy.127
  875.2 4.3 fusion.28
  882.8 6.3 psum.7
  (119 shorter events, 68.0 us)
Async XLA Ops:
  7.2 797.8 %copy-start = (f32[128]{0:T(128)S(1)}, f32[128]{0:T(128)}, u32[]{:S(2)}) copy-start(f32[128]{0:T(128)} %param.28) | copy-start | bytes 1540
  7.2 718.9 %all-gather.2.cloned.1.call-start = ((), (), s32[]{:S(2)}) async-start(), calls=%async_computation.2 | async-start | bytes 1310720 | tf_op jit(solution)/shard_map/all_gather | solution.py:150
  7.9 9.9 %copy-start.9 = (f32[4,2,512]{2,1,0:T(2,128)S(1)}, f32[4,2,512]{2,1,0:T(2,128)}, u32[]{:S(2)}) copy-start(f32[4,2,512]{2,1,0:T(2,128)} %param.23) | copy-start | bytes 49156
  13.0 786.3 %all-to-all-start.1 = ((bf16[2,512,1024]{2,0,1:T(2,128)(2,1)}), bf16[2,512,1024]{2,0,1:T(2,128)(2,1)}, u32[]{:S(2)}, u32[]{:S(2)}) async-start(bf16[2,512,1024]{2,0,1:T(2,128)(2,1)} %copy.128), calls=%async_computation.1 | async-start | bytes 4194304 | tf_op jit(solution)/shard_map/all_to_all | solution.py:111
  29.8 1.6 copy-start.10
  29.8 1.6 copy-start.6
  34.2 3.0 copy-start.15
  34.2 3.0 copy-start.7
  34.2 3.0 copy-start.8
  34.2 3.0 copy-start.13
  40.1 2.0 copy-start.1
  689.4 2.0 copy-start.4
  709.1 5.3 copy-start.2
  709.1 6.4 copy-start.5
  715.5 10.6 %copy-start.14 = (s32[2]{0:T(128)S(1)}, s32[2]{0:T(128)}, u32[]{:S(2)}) copy-start(s32[2]{0:T(128)} %param.26) | copy-start | bytes 28
  799.3 5.3 copy-start.11
  799.3 5.4 copy-start.12
  799.3 54.0 %all-to-all-start = ((f32[2,512,1024]{2,0,1:T(2,128)}), f32[2,512,1024]{2,0,1:T(2,128)}, u32[]{:S(2)}, u32[]{:S(2)}) async-start(f32[2,512,1024]{2,0,1:T(2,128)} %reshape.212), calls=%async_computation | async-start | bytes 8388608 | tf_op jit(solution)/shard_map/all_to_all | solution.py:110
  856.9 1.9 copy-start.3
Sparse Core Ops, SparseCore 0:
  9.6 30.6 all-gather.1
where the time goes:
time: 900 us; the launch traced here: 896 us
  other arithmetic  660 us (73%)
  local copies, waits for them, and re-layouts  87.1 us (10%)
  matrix products  75.6 us (8%)
  waiting for transfers between devices  42.4 us (5%)
  between operations  14.8 us (2%)
  starting transfers between devices  10.1 us (1%)
    another operation x2, other arithmetic, delta_blocks(): jax.scipy.linalg.solve_triangular(system, right, lower=True, unit_diagona...  630 us
    all_to_all x1, waiting for transfers between devices, shuffle_pair(): lax.all_to_all(core, ('head', 'sub'), split_axis=1, concat_axis=2, tiled=...  41.7 us
  transfers between devices with their start and end apart: 3, of which 1 were waited for; matrix products, arithmetic and copies ran while one was open for 88% of the time, Pallas kernels for 0%

commit v1 on v0

--- a/solution.py
+++ b/solution.py
@@ -107,7 +107,15 @@
 
 def shuffle_pair(core, gate):
     moved_core, moved_gate = (
-        lax.all_to_all(core, ("head", "sub"), split_axis=1, concat_axis=2, tiled=True),
+        jnp.concatenate(
+            lax.all_to_all(
+                jnp.stack(jnp.split(core, lax.axis_size(("head", "sub")), axis=1)),
+                ("head", "sub"),
+                0,
+                0,
+            ),
+            axis=2,
+        ),
         lax.all_to_all(
             gate.astype(jnp.float32), ("head", "sub"), split_axis=1, concat_axis=2, tiled=True
         ).astype(gate.dtype),

time: 900 us -> 901 us (level)
  no operation moved by 1% of the time
where the time goes in v1:
time: 901 us; the launch traced here: 896 us
  other arithmetic  664 us (74%)
  local copies, waits for them, and re-layouts  83.1 us (9%)
  matrix products  75.6 us (8%)
  waiting for transfers between devices  42.4 us (5%)
  between operations  14.8 us (2%)
  starting transfers between devices  9.99 us (1%)
    another operation x2, other arithmetic, delta_blocks(): jax.scipy.linalg.solve_triangular(system, right, lower=True, unit_diagona...  630 us
    all_to_all x1, waiting for transfers between devices, shuffle_pair(): lax.all_to_all(jnp.stack(jnp.split(core, lax.axis_size(('head', 'sub')),...  41.7 us
  transfers between devices with their start and end apart: 3, of which 1 were waited for; matrix products, arithmetic and copies ran while one was open for 88% of the time, Pallas kernels for 0%

profile of v1, /device:TPU:0, one launch (start us, length us, event | category | flops | bytes accessed | tf_op | source)
XLA Modules:
  0.0 896.5 jit_solution(10230409666183119312)
XLA Ops:
  7.9 5.1 copy.125
  13.0 4.8 all-to-all-start.1
  17.9 3.3 reshape.200
  21.2 2.8 divide_multiply_fusion.1
  31.4 2.8 divide_multiply_fusion
  34.2 2.9 copy.138
  42.1 11.1 %add_bitcast_fusion = f32[4,2,8,1,128,128]{5,4,3,2,1,0:T(8,128)} fusion(f32[128,128]{1,0:T(8,128)S(1)} %get-tuple-element.153, f32[4,2,8,128]{3,2,1,0:T(8,128)S(1)} %reduce_window_sum.11, f32[4,2,8,128]{3,2,1,0:T(8,128)S(1)} %copy_bitcast_fusion, f32[128,128]{1,0:T(8,128)S(1)} %get-tuple-element.152, pred[128,128]{1,0:T(8,128)(4,1)S(1)} %iota_compare_fusion.1, ...), kind=kOutput, calls=%fused_computation.45 | convolution fusion | flops 1620049920 | bytes 8634368 | tf_op jit(solution)/shard_map/nshid,nshjd->nshij/dot_general | solution.py:52
  53.2 630.3 %custom-call.4 = f32[4,2,8,1,128,128]{4,5,3,2,1,0:T(8,128)} custom-call(f32[4,2,8,1,128,128]{5,4,3,2,1,0:T(8,128)} %add_bitcast_fusion), custom_call_target="InvertDiagBlocksLowerTriangular" | custom-call | tf_op jit(solution)/shard_map/jit(_solve_triangular)/vmap(vmap(vmap()))/triangular_solve | solution.py:60
  693.6 5.2 bitcast_multiply_fusion.3
  698.8 10.3 %fusion.12 = f32[4,2,8,128,256]{4,3,2,1,0:T(8,128)S(1)} fusion(f32[4,2,8,128,128]{4,3,2,1,0:T(8,128)S(1)} %get-tuple-element.155, f32[4,2,8,128,128]{4,3,2,1,0:T(8,128)S(1)} %get-tuple-element.154, f32[4,2,8,1,128,128]{4,5,3,2,1,0:T(8,128)} %custom-call.4), kind=kOutput, calls=%fused_computation.23 | convolution fusion | flops 3223322624 | bytes 20971520 | tf_op jit(solution)/shard_map/jit(_solve_triangular)/vmap(vmap(vmap()))/triangular_solve | solution.py:60
  709.1 5.3 fusion.48
  715.5 10.6 %fusion.27 = f32[4,2,8,128,128]{4,3,2,1,0:T(8,128)} fusion(f32[4,2,8,128]{3,2,1,0:T(8,128)S(1)} %reduce_window_sum.11, pred[128,128]{1,0:T(8,128)(4,1)S(1)} %iota_compare_fusion.1, f32[2,4,128,8,128]{4,2,1,3,0:T(8,128)S(1)} %bitcast.185, f32[4,2,8,128,128]{4,3,0,2,1:T(8,128)S(1)} %bitcast.187), kind=kOutput, calls=%fused_computation.47 | convolution fusion | flops 1614807040 | bytes 12632064 | tf_op jit(solution)/shard_map/nshid,nshjd->nshij/dot_general | solution.py:63
  728.4 58.6 %while.13 = (s32[]{:T(128)}, f32[2,8,128,128]{3,2,1,0:T(8,128)S(1)}, f32[4,2,8,128,128]{4,3,2,1,0:T(8,128)}, f32[4,2,8,128]{3,2,1,0:T(8,128)S(1)}, f32[4,2,8,128...) while((s32[]{:T(128)}, ...), condition=%wide.region_4.5_spmd.clone, body=%wide.region_3.4_spmd.sunk.clone | while | flops 1612187648 | bytes 20032420 | solution.py:79
  731.3 2.8 convolution_subtract_fusion.3
  734.1 3.4 fusion.82
  745.9 2.8 convolution_subtract_fusion.3
  748.7 3.4 fusion.82
  760.6 2.8 convolution_subtract_fusion.3
  763.4 3.4 fusion.82
  775.2 2.8 convolution_subtract_fusion.3
  778.0 3.4 fusion.82
  787.0 6.5 copy.122
  793.5 4.9 reshape.204
  803.2 5.2 all-to-all-start
  808.7 6.8 copy.126
  815.5 41.7 %all-to-all-done = f32[4,2,128,1024]{3,2,1,0:T(8,128)} async-done(((f32[4,2,128,1024]{3,2,1,0:T(8,128)}), f32[4,2,128,1024]{3,2,1,0:T(8,128)}, u32[]{:S(2)}, u32[]{:S(2)}) %all-to-all-start) | async-done | bytes 4194336 | tf_op jit(solution)/shard_map/all_to_all | solution.py:111
  857.2 5.0 bitcast_multiply_fusion.5
  862.1 5.4 copy.124
  870.2 5.4 copy.123
  875.6 4.3 fusion.28
  880.4 2.7 copy.127
  883.1 6.3 psum.7
  (118 shorter events, 68.1 us)
Async XLA Ops:
  7.2 801.5 %copy-start = (f32[128]{0:T(128)S(1)}, f32[128]{0:T(128)}, u32[]{:S(2)}) copy-start(f32[128]{0:T(128)} %param.28) | copy-start | bytes 1540
  7.2 718.9 %all-gather.2.cloned.1.call-start = ((), (), s32[]{:S(2)}) async-start(), calls=%async_computation.2 | async-start | bytes 1310720 | tf_op jit(solution)/shard_map/all_gather | solution.py:158
  7.9 9.9 %copy-start.8 = (f32[4,2,512]{2,1,0:T(2,128)S(1)}, f32[4,2,512]{2,1,0:T(2,128)}, u32[]{:S(2)}) copy-start(f32[4,2,512]{2,1,0:T(2,128)} %param.23) | copy-start | bytes 49156
  13.0 790.2 %all-to-all-start.1 = ((bf16[2,512,1024]{2,0,1:T(2,128)(2,1)}), bf16[2,512,1024]{2,0,1:T(2,128)(2,1)}, u32[]{:S(2)}, u32[]{:S(2)}) async-start(bf16[2,512,1024]{2,0,1:T(2,128)(2,1)} %copy.125), calls=%async_computation.1 | async-start | bytes 4194304 | tf_op jit(solution)/shard_map/all_to_all | solution.py:119
  29.8 1.6 copy-start.9
  29.8 1.6 copy-start.5
  34.2 3.0 copy-start.14
  34.2 3.0 copy-start.6
  34.2 3.0 copy-start.7
  34.2 3.0 copy-start.12
  40.1 2.0 copy-start.1
  689.4 2.0 copy-start.3
  709.1 5.3 copy-start.2
  709.1 6.4 copy-start.4
  715.5 10.6 %copy-start.13 = (s32[2]{0:T(128)S(1)}, s32[2]{0:T(128)}, u32[]{:S(2)}) copy-start(s32[2]{0:T(128)} %param.26) | copy-start | bytes 28
  803.1 5.2 copy-start.10
  803.1 5.3 copy-start.11
  803.2 54.0 %all-to-all-start = ((f32[4,2,128,1024]{3,2,1,0:T(8,128)}), f32[4,2,128,1024]{3,2,1,0:T(8,128)}, u32[]{:S(2)}, u32[]{:S(2)}) async-start(f32[4,2,128,1024]{3,2,1,0:T(8,128)} %pad_maximum_fusion), calls=%async_computation | async-start | bytes 8388608 | tf_op jit(solution)/shard_map/all_to_all | solution.py:111
Sparse Core Ops, SparseCore 0:
  9.6 30.6 all-gather.1
